TPU v7x, 32 devices: a whole 2x2x4 slice. The times are simulated.
32 devices in a mesh: group: 2 (over y), lat: 4 (over z), lon: 2 (over x), fld: 2 (over core).
Axes of the slice: x: 2, y: 2, z: 4, core: 2. Of those that a mesh axis runs over, the one named last changes fastest.
Arguments:
- exchange_density_arrays: bfloat16 [24, 336, 1440], P(('group', 'fld'), 'lat', 'lon'), parts along dimension 0, may hold values from -6 to 6
- marine_thermal_frozen_values: float32 [4, 1008, 4320], P(('group', 'fld'), 'lat', 'lon'), parts along dimension 0, may hold values from -6 to 6
- coarse_continent_flag: int32 [336, 1440], P('lat', 'lon'), may hold values 0 or 1
- marine_continent_flag: int32 [1008, 4320], P('lat', 'lon'), may hold values 0 or 1
- parallel_source_initial: int32 [1008], replicated, may hold values from 0 to 332, as said below
- parallel_source_tally: int32 [1008], replicated, may hold values from 1 to 4
- parallel_intersect_coefs: bfloat16 [1008, 4], replicated, may hold values from 0.25 to 1
- meridian_source_displacement: int32 [4320], replicated, may hold values from 0 to 4
- meridian_source_tally: int32 [4320], replicated, may hold values from 1 to 5
- meridian_intersect_coefs: bfloat16 [4320, 5], replicated, may hold values from 0.25 to 1
Outputs:
- ocean_flux: bfloat16 [24, 1008, 4320], P(('group', 'fld'), 'lat', 'lon'), parts along dimension 0
- coarse_boundary_values: float32 [4, 336, 1440], P(('group', 'fld'), 'lat', 'lon'), parts along dimension 0
There are 2 independent parts, one for each index of `group`. A program takes and returns all parts, laid end to end along the dimension named above; an argument that names none is the same for every part. Nothing has to cross between parts.
Inputs may be any that keep to these rules, and one draw needn't show every extreme that they name: `parallel_source_initial`: nondecreasing along the ocean rows; the first entry is 0.
All inputs are finite; a program needn't handle non-finite values. No bound on the sum of `coarse_continent_flag` or of `marine_continent_flag` on one device may be relied on, other than what follows from the above.
Results may differ from a plain program's by a relative error of at most 0.001.
Values may be sent and summed in bfloat16 or wider, within the bound.
A program may use at most 192 MiB of HBM per device.

v0:
```python
import jax
import jax.numpy as jnp
import numpy as np
from jax import lax
from jax.experimental import pallas as pl
from jax.experimental.pallas import tpu as pltpu
from jax.sharding import PartitionSpec as P

LON_REACH = 4
FLOOR_SHARE = 0.25
TILE = 256
LANE = 128
VMEM_LIMIT = 56 * 1024 * 1024


def round_up(value, unit):
    return (value + unit - 1) // unit * unit


def neighbour(block, axis, step):
    count = lax.axis_size(axis)
    return lax.ppermute(block, axis, [(i, (i + step) % count) for i in range(count)])


def shift(block, axis, step):
    count = lax.axis_size(axis)
    pairs = [(i, i + step) for i in range(count) if 0 <= i + step < count]
    return lax.ppermute(block, axis, pairs)


def tap_weights(widths, weights):
    tap_count = weights.shape[1]
    allowed = jnp.arange(tap_count, dtype=jnp.int32)[None, :] < widths[:, None]
    return jnp.where(allowed, weights.astype(jnp.float32), jnp.float32(0.0))


def tile_chunks(atmos_cols, ocean_cols):
    tiles = -(-ocean_cols // TILE)
    chunk_total = round_up(atmos_cols + 2 * LON_REACH + 1, LANE) // LANE
    table = []
    for tile in range(tiles):
        first = tile * TILE
        last = min(first + TILE, ocean_cols) - 1
        slots = range(first // 3 - LON_REACH, last // 3 + LON_REACH + 1)
        chunks = sorted({(s if s >= 0 else atmos_cols + 2 * LON_REACH + s) // LANE for s in slots})
        assert len(chunks) <= 2
        if len(chunks) == 1:
            chunks.append((chunks[0] + 1) % chunk_total)
        table.append(chunks)
    return np.array(table, np.int32), chunk_total


def column_tiles(shift, col_taps, chunk_table, atmos_cols):
    tiles = chunk_table.shape[0]
    cols = shift.shape[0]
    pad = tiles * TILE - cols
    taps = jnp.pad(col_taps, ((0, pad), (0, 0))).T.reshape(-1, tiles, 1, TILE)
    first = jnp.arange(cols, dtype=jnp.int32) // 3 - LON_REACH + shift
    first = jnp.pad(first, (0, pad)).reshape(tiles, 1, TILE)
    slots = chunk_table[:, :, None] * LANE + np.arange(LANE)[None, None, :]
    slots = slots.reshape(tiles, TILE, 1)
    wide = atmos_cols + 2 * LON_REACH
    offset = np.where(slots < atmos_cols + LON_REACH, slots, np.where(slots < wide, slots - wide, -100))
    offset = jnp.asarray(offset.astype(np.int32))
    result = jnp.zeros((tiles, TILE, TILE), jnp.float32)
    for k in range(col_taps.shape[1]):
        result = result + jnp.where(offset == first + k, taps[k], jnp.float32(0.0))
    return result.astype(jnp.bfloat16)


def row_matrix(first_row, row_taps, atmos_total):
    index = jnp.arange(atmos_total, dtype=jnp.int32)[None, :]
    result = jnp.zeros((first_row.shape[0], atmos_total), jnp.float32)
    for k in range(row_taps.shape[1]):
        result = result + jnp.where(index == (first_row + k)[:, None], row_taps[:, k][:, None], 0.0)
    return result


def split(value):
    high = value.astype(jnp.bfloat16)
    low = (value - high.astype(jnp.float32)).astype(jnp.bfloat16)
    return high, low


def forward_kernel(blocks, chunk_ref, *refs):
    x_refs, p_refs = refs[:blocks], refs[blocks : 2 * blocks]
    q_ref, rows_ref, flag_ref, out_ref, high_ref, low_ref = refs[2 * blocks :]
    tile = pl.program_id(0)
    channels = x_refs[0].shape[0]
    chunk_total = high_ref.shape[0]
    ocean_rows = flag_ref.shape[1]

    @pl.when(tile == 0)
    def _():
        for ch in range(channels):
            value = None
            for x_ref, p_ref in zip(x_refs, p_refs):
                part = jnp.dot(p_ref[...], x_ref[ch], preferred_element_type=jnp.float32)
                value = part if value is None else value + part
            high, low = split(value.T)
            for c in range(chunk_total):
                high_ref[c, ch] = high[c * LANE : (c + 1) * LANE]
                low_ref[c, ch] = low[c * LANE : (c + 1) * LANE]

    first, second = chunk_ref[2 * tile], chunk_ref[2 * tile + 1]
    weights = q_ref[0].astype(jnp.float32).T
    col_sums = jnp.sum(weights, axis=1, keepdims=True)
    weights = weights.astype(jnp.bfloat16)

    def spread(ch):
        high = jnp.concatenate([high_ref[first, ch], high_ref[second, ch]], axis=0)
        low = jnp.concatenate([low_ref[first, ch], low_ref[second, ch]], axis=0)
        value = jnp.dot(weights, high, preferred_element_type=jnp.float32)
        value = value + jnp.dot(weights, low, preferred_element_type=jnp.float32)
        return value[:, :ocean_rows]

    floor = FLOOR_SHARE * rows_ref[...] * col_sums
    water = (1 - flag_ref[...]).astype(jnp.float32)
    factor = water / jnp.maximum(spread(channels - 1), floor)
    for ch in range(channels - 1):
        out_ref[ch] = (spread(ch) * factor).astype(out_ref.dtype)


def forward_call(pieces, matrices, q, chunk_table, chunk_total, row_sums, flag):
    blocks = len(pieces)
    channels = pieces[0].shape[0]
    rows_padded = matrices[0].shape[0]
    ocean_cols, ocean_rows = flag.shape
    tiles = q.shape[0]
    whole = lambda array: pl.BlockSpec(array.shape, lambda j, *_: (0,) * array.ndim)
    return pl.pallas_call(
        lambda *refs: forward_kernel(blocks, *refs),
        out_shape=jax.ShapeDtypeStruct((channels - 1, ocean_cols, ocean_rows), jnp.bfloat16),
        grid_spec=pltpu.PrefetchScalarGridSpec(
            num_scalar_prefetch=1,
            grid=(tiles,),
            in_specs=[whole(array) for array in (*pieces, *matrices)]
            + [
                pl.BlockSpec((1, TILE, TILE), lambda j, *_: (j, 0, 0)),
                whole(row_sums),
                pl.BlockSpec((TILE, ocean_rows), lambda j, *_: (j, 0)),
            ],
            out_specs=pl.BlockSpec((channels - 1, TILE, ocean_rows), lambda j, *_: (0, j, 0)),
            scratch_shapes=[
                pltpu.VMEM((chunk_total, channels, LANE, rows_padded), jnp.bfloat16),
                pltpu.VMEM((chunk_total, channels, LANE, rows_padded), jnp.bfloat16),
            ],
        ),
        compiler_params=pltpu.CompilerParams(vmem_limit_bytes=VMEM_LIMIT),
        cost_estimate=pl.CostEstimate(
            flops=2 * channels * rows_padded * 2 * TILE * tiles * TILE,
            bytes_accessed=16 * 1024 * 1024,
            transcendentals=0,
        ),
        name="spread_fluxes",
    )(jnp.asarray(chunk_table.reshape(-1)), *pieces, *matrices, q, row_sums, flag)


def backward_kernel(blocks, sizes, chunk_ref, field_ref, flag_ref, q_ref, *refs):
    ocean_rows, ocean_cols, wide = sizes
    matrix_refs, out_refs = refs[:blocks], refs[blocks : 2 * blocks]
    ones_ref, sum_ref = refs[2 * blocks :]
    tile = pl.program_id(0)
    chunk_total = sum_ref.shape[0]

    @pl.when(tile == 0)
    def _():
        lanes = lax.broadcasted_iota(jnp.int32, sum_ref.shape[1:], 2)
        for c in range(chunk_total):
            sum_ref[c] = jnp.where(lanes + c * LANE == wide, 1.0, 0.0)

    row = lax.broadcasted_iota(jnp.int32, field_ref.shape, 0)
    col = lax.broadcasted_iota(jnp.int32, field_ref.shape, 1)
    inside = col < ocean_cols - tile * TILE
    dry = flag_ref[...].astype(jnp.float32).T
    wet = inside & (row < ocean_rows) & (dry == 0.0)
    high, low = split(jnp.where(wet, field_ref[...], 0.0))
    water = jnp.where(wet | (inside & (row >= ocean_rows)), 1.0, 0.0).astype(jnp.bfloat16)
    weights = q_ref[0]

    def fold(value):
        return lax.dot_general(
            value, weights, (((1,), (1,)), ((), ())), preferred_element_type=jnp.float32
        )

    first, second = chunk_ref[2 * tile], chunk_ref[2 * tile + 1]
    for ch, value in enumerate((fold(high) + fold(low), fold(water))):
        sum_ref[first, ch] += value[:, :LANE]
        sum_ref[second, ch] += value[:, LANE:]

    @pl.when(tile == pl.num_programs(0) - 1)
    def _():
        for c in range(chunk_total):
            lanes = slice(c * LANE, (c + 1) * LANE)
            ones_ref[:, lanes] = sum_ref[c, 1, ocean_rows : ocean_rows + 1, :]
            for ch in range(2):
                high, low = split(sum_ref[c, ch])
                for matrix_ref, out_ref in zip(matrix_refs, out_refs):
                    matrix = matrix_ref[...]
                    total = jnp.dot(matrix, high, preferred_element_type=jnp.float32)
                    total = total + jnp.dot(matrix, low, preferred_element_type=jnp.float32)
                    out_ref[ch, :, lanes] = total


def backward_call(field, flag, q, matrices, chunk_table, chunk_total, wide):
    ocean_cols, ocean_rows = flag.shape
    rows_padded = matrices[0].shape[1]
    blocks = len(matrices)
    tiles = q.shape[0]
    width = chunk_total * LANE
    shapes = [(2, matrix.shape[0], width) for matrix in matrices] + [(1, width)]
    whole = lambda shape: pl.BlockSpec(shape, lambda j, *_: (0,) * len(shape))
    return pl.pallas_call(
        lambda *refs: backward_kernel(blocks, (ocean_rows, ocean_cols, wide), *refs),
        out_shape=[jax.ShapeDtypeStruct(shape, jnp.float32) for shape in shapes],
        grid_spec=pltpu.PrefetchScalarGridSpec(
            num_scalar_prefetch=1,
            grid=(tiles,),
            in_specs=[
                pl.BlockSpec((rows_padded, TILE), lambda j, *_: (0, j)),
                pl.BlockSpec((TILE, rows_padded), lambda j, *_: (j, 0)),
                pl.BlockSpec((1, TILE, TILE), lambda j, *_: (j, 0, 0)),
            ]
            + [whole(matrix.shape) for matrix in matrices],
            out_specs=[whole(shape) for shape in shapes],
            scratch_shapes=[pltpu.VMEM((chunk_total, 2, rows_padded, LANE), jnp.float32)],
        ),
        compiler_params=pltpu.CompilerParams(vmem_limit_bytes=VMEM_LIMIT),
        cost_estimate=pl.CostEstimate(
            flops=2 * 3 * rows_padded * TILE * tiles * TILE,
            bytes_accessed=8 * 1024 * 1024,
            transcendentals=0,
        ),
        name="fold_surface",
    )(jnp.asarray(chunk_table.reshape(-1)), field, flag, q, *matrices)


def exchange_plan(capacity, rows, stack, field, flag_t, q, first_row, row_taps, row_sums, table):
    chunk_table, chunk_total, atmos_cols = table
    reach = LON_REACH
    wide = atmos_cols + 2 * reach
    steps = -(-capacity // rows)
    tail = capacity - rows * (steps - 1)
    count = lambda t: tail if t == steps else rows

    around = {0: (0, rows)}
    pieces = {0: stack}
    for t in range(1, steps + 1):
        n = count(t)
        around[-t] = (-t * rows + rows - n, n)
        around[t] = (t * rows, n)
        pieces[-t] = shift(pieces[1 - t][:, rows - n :], "lat", 1)
        pieces[t] = shift(pieces[t - 1][:, :n], "lat", -1)
    order = sorted(around)
    matrices = {d: row_matrix(first_row - around[d][0], row_taps, around[d][1]) for d in order}

    *parts, ones = backward_call(
        field,
        flag_t,
        q,
        [matrices[d].T.astype(jnp.bfloat16) for d in order],
        chunk_table,
        chunk_total,
        wide,
    )

    def beside(start):
        edge = [part[:, :, start : start + reach] for part in parts]
        edge.append(jnp.broadcast_to(ones[None, :, start : start + reach], (2, 1, reach)))
        return jnp.concatenate(edge, axis=1)

    from_left = neighbour(beside(atmos_cols), "lon", 1)
    from_right = neighbour(beside(atmos_cols + reach), "lon", -1)
    width = parts[0].shape[2]

    def settle(part, row, n):
        low = from_left[:, row : row + n]
        high = from_right[:, row : row + n]
        rest = ((0, 0), (0, 0))
        return (
            part
            + jnp.pad(low, rest + ((0, width - reach),))
            + jnp.pad(high, rest + ((atmos_cols - reach, width - atmos_cols),))
        )

    totals, row = {}, 0
    for d, part in zip(order, parts):
        totals[d] = settle(part, row, part.shape[1])
        row += part.shape[1]
    lon_sums = settle(jnp.broadcast_to(ones[None], (2, 1, width)), row, 1)[0, 0, :atmos_cols]

    up, down = totals[steps], totals[-steps]
    for t in range(1, steps + 1):
        up, down = shift(up, "lat", 1), shift(down, "lat", -1)
        if t < steps:
            up = totals[steps - t] + jnp.pad(up, ((0, 0), (0, rows - up.shape[1]), (0, 0)))
            down = totals[t - steps] + jnp.pad(down, ((0, 0), (rows - down.shape[1], 0), (0, 0)))
    up = jnp.pad(up, ((0, 0), (0, rows - up.shape[1]), (0, 0)))
    down = jnp.pad(down, ((0, 0), (rows - down.shape[1], 0), (0, 0)))
    total = totals[0] + up + down

    ocean_flux = forward_call(
        [pieces[d] for d in order],
        [matrices[d].astype(jnp.bfloat16) for d in order],
        q,
        chunk_table,
        chunk_total,
        row_sums,
        flag_t,
    )
    lat_sums = total[1, :, wide]
    safe_surface = jnp.maximum(
        total[1, :, :atmos_cols], FLOOR_SHARE * (lat_sums[:, None] * lon_sums[None, :] + 1.0)
    )
    return ocean_flux, total[0, :, :atmos_cols] / safe_surface


def capacities_below(rows):
    return (rows, 2 * rows)


def local(
    exchange_density_arrays,
    marine_thermal_frozen_values,
    coarse_continent_flag,
    marine_continent_flag,
    parallel_source_initial,
    parallel_source_tally,
    parallel_intersect_coefs,
    meridian_source_displacement,
    meridian_source_tally,
    meridian_intersect_coefs,
):
    band_pos = lax.axis_index("lat")
    tile_pos = lax.axis_index("lon")
    bands = lax.axis_size("lat")
    atmos_rows, atmos_cols = coarse_continent_flag.shape
    ocean_rows, ocean_cols = marine_continent_flag.shape
    reach = LON_REACH
    chunk_table, chunk_total = tile_chunks(atmos_cols, ocean_cols)
    width = chunk_total * LANE

    water_atmos = (1 - coarse_continent_flag).astype(jnp.bfloat16)
    stack = jnp.concatenate(
        [exchange_density_arrays * water_atmos[None], water_atmos[None]], axis=0
    )
    channels = stack.shape[0]
    right = neighbour(stack[:, :, :reach], "lon", -1)
    left = neighbour(stack[:, :, atmos_cols - reach :], "lon", 1)
    filler = jnp.zeros((channels, atmos_rows, width - atmos_cols - 2 * reach), jnp.bfloat16)
    stack = jnp.concatenate([stack, right, left, filler], axis=2)

    here = lambda array, pos, count: lax.dynamic_slice_in_dim(array, pos * count, count)
    row_taps = tap_weights(
        here(parallel_source_tally, band_pos, ocean_rows),
        here(parallel_intersect_coefs, band_pos, ocean_rows),
    )
    col_taps = tap_weights(
        here(meridian_source_tally, tile_pos, ocean_cols),
        here(meridian_intersect_coefs, tile_pos, ocean_cols),
    )
    q = column_tiles(
        here(meridian_source_displacement, tile_pos, ocean_cols), col_taps, chunk_table, atmos_cols
    )
    row_sums = jnp.sum(row_taps, axis=1)[None, :]
    rows_padded = round_up(ocean_rows + 1, LANE)
    row_taps = jnp.pad(row_taps, ((0, rows_padded - ocean_rows), (0, 0)))
    first_row = here(parallel_source_initial, band_pos, ocean_rows) - band_pos * atmos_rows
    first_row = jnp.pad(first_row, (0, rows_padded - ocean_rows))

    starts = parallel_source_initial.reshape(bands, ocean_rows)
    band = jnp.arange(bands, dtype=jnp.int32)
    below = jnp.max(band * atmos_rows - starts[:, 0])
    above = jnp.max(starts[:, -1] + row_taps.shape[1] - (band + 1) * atmos_rows)
    need = jnp.maximum(below, above)
    longest = (bands - 1) * atmos_rows
    capacities = sorted({min(n, longest) for n in capacities_below(atmos_rows)} | {longest})
    choice = sum((need > n).astype(jnp.int32) for n in capacities[:-1])

    table = (chunk_table, chunk_total, atmos_cols)
    plans = [
        (lambda *operands, n=n: exchange_plan(n, atmos_rows, *operands, table)) for n in capacities
    ]
    ocean_flux, surface = lax.switch(
        choice,
        plans,
        stack,
        marine_thermal_frozen_values[0],
        marine_continent_flag.T,
        q,
        first_row,
        row_taps,
        row_sums,
    )
    return ocean_flux.transpose(0, 2, 1), surface[None]


def solution(mesh):
    fields = P(("group", "fld"), "lat", "lon")
    cells = P("lat", "lon")
    return jax.shard_map(
        local,
        mesh=mesh,
        in_specs=(fields, fields, cells, cells) + (P(),) * 6,
        out_specs=(fields, fields),
        check_vma=False,
    )
```

profile of v0, /device:TPU:0, one launch (start us, length us, event | category | flops | bytes accessed | tf_op | source)
XLA Modules:
  0.0 105.6 jit_solution(9399391968886859851)
XLA Ops:
  2.7 1.2 %broadcast_multiply_fusion = bf16[6,84,720]{2,1,0:T(8,128)(2,1)S(1)} fusion(bf16[6,84,720]{2,1,0:T(8,128)(2,1)} %param.20, bf16[84,720]{1,0:T(8,128)(2,1)S(1)} %subtract_convert_fusion), kind=kLoop, calls=%fused_computation.271 | loop fusion | flops 362880 | bytes 1572480 | tf_op jit(solution)/shard_map/mul | solution.py:345
  5.6 2.9 %collective-permute-start.30 = (bf16[7,84,4]{2,1,0:T(8,128)(2,1)}, bf16[7,84,4]{2,1,0:T(8,128)(2,1)}, u32[]{:S(2)}, u32[]{:S(2)}) collective-permute-start(bf16[7,84,4]{2,1,0:T(8,128)(2,1)} %get-tuple-element.484), channel_id=1, source_target_pairs={{0,2},{2,0},{1,3},{3,1},{4,6},{6,4},{5,7},{7,5},{8,10},{10,8},{9,1... | collective-permute-start | bytes 14120 | tf_op jit(solution)/shard_map/ppermute | solution.py:22
  14.9 2.4 %add_convert_fusion.30 = bf16[9,256,256]{2,1,0:T(8,128)(2,1)S(1)} fusion(f32[9,256]{1,0:T(8,128)} %broadcast_in_dim.560, s32[9,256]{1,0:T(8,128)} %get-tuple-element.487, f32[9,256]{1,0:T(8,128)} %broadcast_in_dim.558, s32[9,256]{1,0:T(8,128)} %get-tuple-element.488, f32[9,256]{1,0:T(8,128)} %broadcast_in_dim.556, s32[9,256]{1,0:T(8,128)} %get-tuple-element.489, ...), kind=kLoop, calls=%fused_computation.269 | loop fusion | flops 8847360 | bytes 1281024 | tf_op jit(solution)/shard_map/convert_element_type | solution.py:68
  17.3 1.4 %subtract_reduce_fusion = (s32[]{:T(128)}, s32[]{:T(128)}) fusion(s32[4]{0:T(128)S(1)} %get-tuple-element.307, s32[4]{0:T(128)} %get-tuple-element.308), kind=kLoop, calls=%fused_computation.301 | loop fusion | flops 26 | bytes 40 | tf_op jit(solution)/shard_map/reduce_max | solution.py:374
  20.1 2.5 %maximum_maximum_fusion = bf16[7,84,768]{2,1,0:T(8,128)(2,1)} fusion(bf16[7,84,4]{2,1,0:T(8,128)(2,1)} %collective-permute-done.31, bf16[7,84,4]{2,1,0:T(8,128)(2,1)} %collective-permute-done.30, bf16[1,84,720]{2,1,0:T(8,128)(2,1)S(1)} %fusion.33, bf16[6,84,720]{2,1,0:T(8,128)(2,1)} %copy-done.1, bf16[768]{0:T(1024)(128)(2,1)S(1)} %pad.150.clone), kind=kLoop, calls=%fused_computation.270 | loop fusion | flops 4515840 | bytes 1760832 | tf_op jit(solution)/shard_map/concatenate | solution.py:351
  22.7 82.2 %conditional.1 = (bf16[6,2160,252]{2,1,0:T(8,128)(2,1)}, f32[1,84,720]{2,0,1:T(1,128)S(1)}) conditional(s32[]{:T(128)} %clamp.3, (bf16[7,84,768]{2,1,0:T(8,128)(2,1)}, s32[1008]{0:T(1024)S(1)}, f32[252,4]{0,1:T(4,128)S(1)}, (), bf16[9,256,256]{2,1,0:T(8,128)(2,1)S(1)}, /*index=5*/f32[252,4]{0,1:T(4,128)S(1)}, ...), branch_computations={%region_3.4_spmd, %region_4.5_spmd, %region_5.6_spmd} | conditional | flops 5140333568 | bytes 86950768 | solution.py:384
  22.8 3.1 %copy.285 = f32[1,252,2160]{2,1,0:T(8,128)} copy(f32[1,252,2160]{2,0,1:T(1,128)} %get-tuple-element.284) | data formatting | bytes 4354560 | tf_op jit(solution)/shard_map/squeeze | solution.py:388
  26.6 9.8 %fold_surface.3 = (f32[2,84,768]{2,1,0:T(8,128)}, f32[2,84,768]{2,1,0:T(8,128)}, f32[2,84,768]{2,1,0:T(8,128)}, f32[1,768]{1,0:T(1,128)}) custom-call(s32[18]{0:T(128)} %constant.209.clone.1.refs_0_, f32[252,2160]{1,0:T(8,128)} %bitcast.51, s32[2160,252]{1,0:T(8,128)S(1)} %get-tuple-element.61.refs_9_.refs_2_, ...), custom_call_target="tpu_custom_call" | custom-call | flops 905969664 | bytes 8388608 | tf_op jit(solution)/shard_map/cond/branch_0_fun/fold_surface/pallas_call | solution.py:213
  37.2 1.1 %fusion.14 = (f32[2,84,4]{2,1,0:T(8,128)S(1)}, f32[2,84,4]{2,1,0:T(8,128)S(1)}) fusion(f32[2,84,768]{2,1,0:T(8,128)} %get-tuple-element.66), kind=kLoop, calls=%fused_computation.305 | loop fusion | bytes 10752 | tf_op jit(solution)/shard_map/cond/branch_0_fun/slice | solution.py:268
  38.3 1.2 %fusion.12 = (f32[2,84,4]{2,1,0:T(8,128)S(1)}, f32[2,84,4]{2,1,0:T(8,128)S(1)}, f32[2,84,4]{2,1,0:T(8,128)S(1)}, f32[2,84,4]{2,1,0:T(8,128)S(1)}) fusion(f32[2,84,768]{2,1,0:T(8,128)} %get-tuple-element.65, f32[2,84,768]{2,1,0:T(8,128)} %get-tuple-element.64), kind=kLoop, calls=%fused_computation.303 | loop fusion | bytes 21504 | tf_op jit(solution)/shard_map/cond/branch_0_fun/slice | solution.py:268
  39.5 2.1 %collective-permute-start.3 = (f32[2,253,4]{2,1,0:T(8,128)S(1)}, f32[2,253,4]{2,1,0:T(8,128)S(1)}, u32[]{:S(2)}, u32[]{:S(2)}) collective-permute-start(f32[2,253,4]{2,1,0:T(8,128)S(1)} %pad_maximum_fusion.1), channel_id=1, source_target_pairs={{0,2},{2,0},{1,3},{3,1},{4,6},{6,4},{5,7},{7,5},{8,10},{10,8},{9,1... | collective-permute-start | bytes 24296 | tf_op jit(solution)/shard_map/cond/branch_0_fun/ppermute | solution.py:22
  41.7 7.1 %collective-permute-done.3 = f32[2,253,4]{2,1,0:T(8,128)S(1)} collective-permute-done((f32[2,253,4]{2,1,0:T(8,128)S(1)}, f32[2,253,4]{2,1,0:T(8,128)S(1)}, u32[]{:S(2)}, u32[]{:S(2)}) %collective-permute-start.3) | collective-permute-done | bytes 8128 | tf_op jit(solution)/shard_map/cond/branch_0_fun/ppermute | solution.py:22
  48.9 4.1 %collective-permute-done.2 = f32[2,253,4]{2,1,0:T(8,128)S(1)} collective-permute-done((f32[2,253,4]{2,1,0:T(8,128)S(1)}, f32[2,253,4]{2,1,0:T(8,128)S(1)}, u32[]{:S(2)}, u32[]{:S(2)}) %collective-permute-start.2) | collective-permute-done | bytes 8128 | tf_op jit(solution)/shard_map/cond/branch_0_fun/ppermute | solution.py:22
  53.9 1.1 %copy.184 = f32[2,84,768]{2,0,1:T(2,128)} copy(f32[2,84,768]{2,1,0:T(8,128)S(1)} %pad_add_fusion.1) | data formatting | bytes 1032192 | tf_op jit(solution)/shard_map/cond/branch_0_fun/add | solution.py:281
  55.0 1.1 copy.186
  56.1 1.3 %collective-permute-start.5 = (f32[2,84,768]{2,0,1:T(2,128)}, f32[2,84,768]{2,0,1:T(2,128)}, u32[]{:S(2)}, u32[]{:S(2)}) collective-permute-start(f32[2,84,768]{2,0,1:T(2,128)} %copy.186), channel_id=1, source_target_pairs={{4,0},{8,4},{12,8},{5,1},{9,5},{13,9},{6,2},{10,6},{14,10},{7,3},{... | collective-permute-start | bytes 1548296 | tf_op jit(solution)/shard_map/cond/branch_0_fun/ppermute | solution.py:28
  57.4 5.4 %collective-permute-start.4 = (f32[2,84,768]{2,0,1:T(2,128)}, f32[2,84,768]{2,0,1:T(2,128)}, u32[]{:S(2)}, u32[]{:S(2)}) collective-permute-start(f32[2,84,768]{2,0,1:T(2,128)} %copy.184), channel_id=1, source_target_pairs={{0,4},{4,8},{8,12},{1,5},{5,9},{9,13},{2,6},{6,10},{10,14},{3,7},{... | collective-permute-start | bytes 1548296 | tf_op jit(solution)/shard_map/cond/branch_0_fun/ppermute | solution.py:28
  62.7 1.3 %collective-permute-start.1 = (bf16[7,84,768]{2,1,0:T(8,128)(2,1)}, bf16[7,84,768]{2,1,0:T(8,128)(2,1)}, u32[]{:S(2)}, u32[]{:S(2)}) collective-permute-start(bf16[7,84,768]{2,1,0:T(8,128)(2,1)} %get-tuple-element.56.refs_2_), channel_id=1, source_target_pairs={{4,0},{8,4},{12,8},{5,1},{9,5},{13,9},{6,2},{10,6},{14,10},{7,3},{... | collective-permute-start | bytes 2709512 | tf_op jit(solution)/shard_map/cond/branch_0_fun/ppermute | solution.py:28
  64.0 5.5 %collective-permute-start = (bf16[7,84,768]{2,1,0:T(8,128)(2,1)}, bf16[7,84,768]{2,1,0:T(8,128)(2,1)}, u32[]{:S(2)}, u32[]{:S(2)}) collective-permute-start(bf16[7,84,768]{2,1,0:T(8,128)(2,1)} %get-tuple-element.56.refs_2_), channel_id=1, source_target_pairs={{0,4},{4,8},{8,12},{1,5},{5,9},{9,13},{2,6},{6,10},{10,14},{3,7},{... | collective-permute-start | bytes 2709512 | tf_op jit(solution)/shard_map/cond/branch_0_fun/ppermute | solution.py:28
  70.8 1.4 %add_convert_fusion = (bf16[256,84]{1,0:T(8,128)(2,1)}, bf16[256,84]{1,0:T(8,128)(2,1)}, bf16[256,84]{1,0:T(8,128)(2,1)}) fusion(s32[256]{0:T(256)S(1)} %get-tuple-element.334, s32[256]{0:T(256)S(1)} %get-tuple-element.335, s32[256]{0:T(256)S(1)} %get-tuple-element.336, s32[256]{0:T(256)S(1)} %get-tuple-element.333, f32[256]{0:T(256)S(1)} %bitcast.104, ...), kind=kLoop, calls=%fused_computation.9 | loop fusion | flops 774144 | bytes 145408 | tf_op jit(solution)/shard_map/cond/branch_0_fun/convert_element_type | solution.py:304
  74.4 1.5 %copy_add_fusion = f32[2,84,768]{2,1,0:T(8,128)S(1)} fusion(f32[2,84,768]{2,0,1:T(2,128)} %collective-permute-done.5, f32[2,84,768]{2,0,1:T(2,128)} %collective-permute-done.4, f32[2,84,4]{2,1,0:T(8,128)S(1)} %get-tuple-element.318, f32[2,84,768]{2,1,0:T(8,128)} %get-tuple-element.64, f32[2,84,4]{2,1,0:T(8,128)} %get-tuple-element.315), kind=kLoop, calls=%fused_computation.1 | loop fusion | flops 516096 | bytes 2069760 | tf_op jit(solution)/shard_map/cond/branch_0_fun/add | solution.py:300
  76.5 14.4 %collective-permute-done.1.refs_3_ = bf16[7,84,768]{2,1,0:T(8,128)(2,1)} collective-permute-done((bf16[7,84,768]{2,1,0:T(8,128)(2,1)}, bf16[7,84,768]{2,1,0:T(8,128)(2,1)}, u32[]{:S(2)}, u32[]{:S(2)}) %collective-permute-start.1) | collective-permute-done | bytes 903200 | tf_op jit(solution)/shard_map/cond/branch_0_fun/ppermute | solution.py:28
  90.9 1.2 %collective-permute-done.refs_1_ = bf16[7,84,768]{2,1,0:T(8,128)(2,1)} collective-permute-done((bf16[7,84,768]{2,1,0:T(8,128)(2,1)}, bf16[7,84,768]{2,1,0:T(8,128)(2,1)}, u32[]{:S(2)}, u32[]{:S(2)}) %collective-permute-start) | collective-permute-done | bytes 903200 | tf_op jit(solution)/shard_map/cond/branch_0_fun/ppermute | solution.py:28
  92.0 12.8 %spread_fluxes.3 = bf16[6,2160,252]{2,1,0:T(8,128)(2,1)} custom-call(s32[18]{0:T(128)} %constant.209.clone.1.refs_0_, bf16[7,84,768]{2,1,0:T(8,128)(2,1)} %collective-permute-done.refs_1_, bf16[7,84,768]{2,1,0:T(8,128)(2,1)} %get-tuple-element.56.refs_2_, bf16[7,84,768]{2,1,0:T(8,128)(2,1)} %collective-permute-done.1.refs_3_, ...), custom_call_target="tpu_custom_call" | custom-call | flops 4227858432 | bytes 16777216 | tf_op jit(solution)/shard_map/cond/branch_0_fun/spread_fluxes/pallas_call | solution.py:131
  (72 shorter events, 17.6 us)
Async XLA Ops:
  0.6 7.9 %copy-start.19 = (s32[1008]{0:T(1024)S(1)}, s32[1008]{0:T(1024)}, u32[]{:S(2)}) copy-start(s32[1008]{0:T(1024)} %param.24) | copy-start | bytes 12100
  0.6 8.7 %copy-start.82 = (s32[4320]{0:T(1024)S(1)}, s32[4320]{0:T(1024)}, u32[]{:S(2)}) copy-start(s32[4320]{0:T(1024)} %param.27) | copy-start | bytes 51844
  0.7 8.8 %copy-start.83 = (s32[4320]{0:T(1024)S(1)}, s32[4320]{0:T(1024)}, u32[]{:S(2)}) copy-start(s32[4320]{0:T(1024)} %param.28) | copy-start | bytes 51844
  0.7 8.8 %copy-start.18 = (bf16[4320,5]{0,1:T(8,128)(2,1)S(1)}, bf16[4320,5]{0,1:T(8,128)(2,1)}, u32[]{:S(2)}) copy-start(bf16[4320,5]{0,1:T(8,128)(2,1)} %param.29) | copy-start | bytes 129604
  3.9 0.9 copy-start.1
  5.6 17.1 %copy-start = (s32[252,2160]{0,1:T(8,128)S(1)}, s32[252,2160]{0,1:T(8,128)}, u32[]{:S(2)}) copy-start(s32[252,2160]{0,1:T(8,128)} %param.23) | copy-start | bytes 6531844
  5.6 14.6 %collective-permute-start.30 = (bf16[7,84,4]{2,1,0:T(8,128)(2,1)}, bf16[7,84,4]{2,1,0:T(8,128)(2,1)}, u32[]{:S(2)}, u32[]{:S(2)}) collective-permute-start(bf16[7,84,4]{2,1,0:T(8,128)(2,1)} %get-tuple-element.484), channel_id=1, source_target_pairs={{0,2},{2,0},{1,3},{3,1},{4,6},{6,4},{5,7},{7,5},{8,10},{10,8},{9,1... | collective-permute-start | bytes 14120 | tf_op jit(solution)/shard_map/ppermute | solution.py:22
  8.5 11.6 %collective-permute-start.31 = (bf16[7,84,4]{2,1,0:T(8,128)(2,1)}, bf16[7,84,4]{2,1,0:T(8,128)(2,1)}, u32[]{:S(2)}, u32[]{:S(2)}) collective-permute-start(bf16[7,84,4]{2,1,0:T(8,128)(2,1)} %get-tuple-element.485), channel_id=1, source_target_pairs={{0,2},{2,0},{1,3},{3,1},{4,6},{6,4},{5,7},{7,5},{8,10},{10,8},{9,1... | collective-permute-start | bytes 14120 | tf_op jit(solution)/shard_map/ppermute | solution.py:22
  36.5 17.3 %copy-start.7 = (f32[2,84,768]{2,1,0:T(8,128)S(1)}, f32[2,84,768]{2,1,0:T(8,128)}, u32[]{:S(2)}) copy-start(f32[2,84,768]{2,1,0:T(8,128)} %get-tuple-element.66) | copy-start | bytes 1548292 | tf_op jit(solution)/shard_map/cond
  39.5 15.5 %copy-start.6 = (f32[2,84,768]{2,1,0:T(8,128)S(1)}, f32[2,84,768]{2,1,0:T(8,128)}, u32[]{:S(2)}) copy-start(f32[2,84,768]{2,1,0:T(8,128)} %get-tuple-element.65) | copy-start | bytes 1548292 | tf_op jit(solution)/shard_map/cond
  39.5 9.3 %collective-permute-start.3 = (f32[2,253,4]{2,1,0:T(8,128)S(1)}, f32[2,253,4]{2,1,0:T(8,128)S(1)}, u32[]{:S(2)}, u32[]{:S(2)}) collective-permute-start(f32[2,253,4]{2,1,0:T(8,128)S(1)} %pad_maximum_fusion.1), channel_id=1, source_target_pairs={{0,2},{2,0},{1,3},{3,1},{4,6},{6,4},{5,7},{7,5},{8,10},{10,8},{9,1... | collective-permute-start | bytes 24296 | tf_op jit(solution)/shard_map/cond/branch_0_fun/ppermute | solution.py:22
  41.6 11.4 %collective-permute-start.2 = (f32[2,253,4]{2,1,0:T(8,128)S(1)}, f32[2,253,4]{2,1,0:T(8,128)S(1)}, u32[]{:S(2)}, u32[]{:S(2)}) collective-permute-start(f32[2,253,4]{2,1,0:T(8,128)S(1)} %pad_maximum_fusion), channel_id=1, source_target_pairs={{0,2},{2,0},{1,3},{3,1},{4,6},{6,4},{5,7},{7,5},{8,10},{10,8},{9,1... | collective-permute-start | bytes 24296 | tf_op jit(solution)/shard_map/cond/branch_0_fun/ppermute | solution.py:22
  48.8 4.9 %copy-start.15 = (f32[2,253,4]{2,1,0:T(8,128)}, f32[2,253,4]{2,1,0:T(8,128)S(1)}, u32[]{:S(2)}) copy-start(f32[2,253,4]{2,1,0:T(8,128)S(1)} %collective-permute-done.3) | copy-start | bytes 24292 | tf_op jit(solution)/shard_map/cond
  53.0 0.8 copy-start.16
  56.1 17.6 %collective-permute-start.5 = (f32[2,84,768]{2,0,1:T(2,128)}, f32[2,84,768]{2,0,1:T(2,128)}, u32[]{:S(2)}, u32[]{:S(2)}) collective-permute-start(f32[2,84,768]{2,0,1:T(2,128)} %copy.186), channel_id=1, source_target_pairs={{4,0},{8,4},{12,8},{5,1},{9,5},{13,9},{6,2},{10,6},{14,10},{7,3},{... | collective-permute-start | bytes 1548296 | tf_op jit(solution)/shard_map/cond/branch_0_fun/ppermute | solution.py:28
  57.4 17.1 %collective-permute-start.4 = (f32[2,84,768]{2,0,1:T(2,128)}, f32[2,84,768]{2,0,1:T(2,128)}, u32[]{:S(2)}, u32[]{:S(2)}) collective-permute-start(f32[2,84,768]{2,0,1:T(2,128)} %copy.184), channel_id=1, source_target_pairs={{0,4},{4,8},{8,12},{1,5},{5,9},{9,13},{2,6},{6,10},{10,14},{3,7},{... | collective-permute-start | bytes 1548296 | tf_op jit(solution)/shard_map/cond/branch_0_fun/ppermute | solution.py:28
  62.7 28.1 %collective-permute-start.1 = (bf16[7,84,768]{2,1,0:T(8,128)(2,1)}, bf16[7,84,768]{2,1,0:T(8,128)(2,1)}, u32[]{:S(2)}, u32[]{:S(2)}) collective-permute-start(bf16[7,84,768]{2,1,0:T(8,128)(2,1)} %get-tuple-element.56.refs_2_), channel_id=1, source_target_pairs={{4,0},{8,4},{12,8},{5,1},{9,5},{13,9},{6,2},{10,6},{14,10},{7,3},{... | collective-permute-start | bytes 2709512 | tf_op jit(solution)/shard_map/cond/branch_0_fun/ppermute | solution.py:28
  64.0 28.0 %collective-permute-start = (bf16[7,84,768]{2,1,0:T(8,128)(2,1)}, bf16[7,84,768]{2,1,0:T(8,128)(2,1)}, u32[]{:S(2)}, u32[]{:S(2)}) collective-permute-start(bf16[7,84,768]{2,1,0:T(8,128)(2,1)} %get-tuple-element.56.refs_2_), channel_id=1, source_target_pairs={{0,4},{4,8},{8,12},{1,5},{5,9},{9,13},{2,6},{6,10},{10,14},{3,7},{... | collective-permute-start | bytes 2709512 | tf_op jit(solution)/shard_map/cond/branch_0_fun/ppermute | solution.py:28
  104.9 0.7 copy-start.17
where the time goes:
time: 107 us; the launch traced here: 106 us
  waiting for transfers between devices  27.5 us (26%)
  Pallas kernels  22.6 us (21%)
  starting transfers between devices  18.6 us (17%)
  other arithmetic  17.9 us (17%)
  local copies, waits for them, and re-layouts  16.6 us (16%)
  between operations  2.12 us (2%)
    ppermute x4, waiting for transfers between devices, shift(): return lax.ppermute(block, axis, pairs)  16.3 us
    ppermute x4, starting transfers between devices, shift(): return lax.ppermute(block, axis, pairs)  13.4 us
    pallas_call x1, Pallas kernels, forward_call(): pl.pallas_call(lambda *refs: forward_kernel(blocks, *refs), out_shape=jax...  12.8 us
    ppermute x4, waiting for transfers between devices, neighbour(): lax.ppermute(block, axis, [(i, (i + step) % count) for i in range(count)])  11.2 us
    pallas_call x1, Pallas kernels, backward_call(): pl.pallas_call(lambda *refs: backward_kernel(blocks, (ocean_rows, ocean_c...  9.83 us
    ppermute x4, starting transfers between devices, neighbour(): lax.ppermute(block, axis, [(i, (i + step) % count) for i in range(count)])  5.13 us
    squeeze x1, local copies, waits for them, and re-layouts, local(): marine_thermal_frozen_values[0]  3.13 us
    broadcast_in_dim x5, local copies, waits for them, and re-layouts, column_tiles(): result = result + jnp.where(offset == first + k, taps[k], jnp.float32(0.0))  3.01 us
  transfers between devices with their start and end apart: 8, of which 5 were waited for; matrix products, arithmetic and copies ran while one was open for 16% of the time, Pallas kernels for 0%

commit v1 on v0

--- a/solution.py
+++ b/solution.py
@@ -192,7 +192,8 @@
     def _():
         for c in range(chunk_total):
             lanes = slice(c * LANE, (c + 1) * LANE)
-            ones_ref[:, lanes] = sum_ref[c, 1, ocean_rows : ocean_rows + 1, :]
+            ones = sum_ref[c, 1, ocean_rows : ocean_rows + 1, :]
+            ones_ref[:, lanes] = jnp.broadcast_to(ones, (8, LANE))
             for ch in range(2):
                 high, low = split(sum_ref[c, ch])
                 for matrix_ref, out_ref in zip(matrix_refs, out_refs):
@@ -208,7 +209,7 @@
     blocks = len(matrices)
     tiles = q.shape[0]
     width = chunk_total * LANE
-    shapes = [(2, matrix.shape[0], width) for matrix in matrices] + [(1, width)]
+    shapes = [(2, matrix.shape[0], width) for matrix in matrices] + [(8, width)]
     whole = lambda shape: pl.BlockSpec(shape, lambda j, *_: (0,) * len(shape))
     return pl.pallas_call(
         lambda *refs: backward_kernel(blocks, (ocean_rows, ocean_cols, wide), *refs),
@@ -235,6 +236,253 @@
     )(jnp.asarray(chunk_table.reshape(-1)), field, flag, q, *matrices)
 
 
+def neighbours_kernel(atmos_cols, stack_ref, to_left_ref, to_right_ref, *refs):
+    part_refs, ones_ref = refs[:3], refs[3]
+    own_ref, below_ref, above_ref, surface_ref = refs[4:8]
+    (edge_left, edge_right, part_left, part_right, ones_left, ones_right) = refs[8:14]
+    (total, sum_below, sum_above, x_send, x_recv, z_send, z_recv) = refs[14:]
+    reach = LON_REACH
+    wide = atmos_cols + 2 * reach
+    width = stack_ref.shape[2]
+    split_at = atmos_cols // LANE * LANE
+    last = pl.ds(split_at, LANE)
+    band, bands = lax.axis_index("lat"), lax.axis_size("lat")
+    block, blocks = lax.axis_index("lon"), lax.axis_size("lon")
+    left = {"lon": lax.rem(block + blocks - 1, blocks)}
+    right = {"lon": lax.rem(block + 1, blocks)}
+    has_above, has_below = band < bands - 1, band > 0
+    above, below = {"lat": band + 1}, {"lat": band - 1}
+    mesh_id = pl.DeviceIdType.MESH
+
+    barrier = pltpu.get_barrier_semaphore()
+    for target in (left, right):
+        pl.semaphore_signal(barrier, inc=1, device_id=target, device_id_type=mesh_id)
+
+    @pl.when(has_above)
+    def _():
+        pl.semaphore_signal(barrier, inc=1, device_id=above, device_id_type=mesh_id)
+
+    @pl.when(has_below)
+    def _():
+        pl.semaphore_signal(barrier, inc=1, device_id=below, device_id_type=mesh_id)
+
+    @pl.when(has_above & has_below)
+    def _():
+        pl.semaphore_wait(barrier, 4)
+
+    @pl.when(jnp.logical_not(has_above & has_below))
+    def _():
+        pl.semaphore_wait(barrier, 3)
+
+    def beside(slot, source, target, device):
+        return pltpu.make_async_remote_copy(
+            src_ref=source,
+            dst_ref=target,
+            send_sem=x_send.at[slot],
+            recv_sem=x_recv.at[slot],
+            device_id=device,
+            device_id_type=mesh_id,
+        )
+
+    def upward(slot, source, target):
+        return pltpu.make_async_remote_copy(
+            src_ref=source,
+            dst_ref=target,
+            send_sem=z_send.at[slot],
+            recv_sem=z_recv.at[slot],
+            device_id=above,
+            device_id_type=mesh_id,
+        )
+
+    def downward(slot, source, target):
+        return pltpu.make_async_remote_copy(
+            src_ref=source,
+            dst_ref=target,
+            send_sem=z_send.at[slot],
+            recv_sem=z_recv.at[slot],
+            device_id=below,
+            device_id_type=mesh_id,
+        )
+
+    edges = [
+        beside(0, to_left_ref, edge_right, left),
+        beside(1, to_right_ref, edge_left, right),
+    ]
+    sums = []
+    for i, part_ref in enumerate(part_refs):
+        sums.append(beside(2 + 2 * i, part_ref.at[:, :, last], part_right.at[i], left))
+        sums.append(beside(3 + 2 * i, part_ref.at[:, :, last], part_left.at[i], right))
+    sums.append(beside(8, ones_ref.at[:, last], ones_right, left))
+    sums.append(beside(9, ones_ref.at[:, last], ones_left, right))
+    first = pl.ds(0, split_at)
+    ups = [
+        lambda: upward(0, stack_ref.at[:, :, first], below_ref.at[:, :, first]),
+        lambda: upward(1, own_ref.at[:, :, last], below_ref.at[:, :, last]),
+        lambda: upward(2, total.at[2], sum_below),
+    ]
+    downs = [
+        lambda: downward(3, stack_ref.at[:, :, first], above_ref.at[:, :, first]),
+        lambda: downward(4, own_ref.at[:, :, last], above_ref.at[:, :, last]),
+        lambda: downward(5, total.at[0], sum_above),
+    ]
+
+    def start(i):
+        @pl.when(has_above)
+        def _():
+            ups[i]().start()
+
+        @pl.when(has_below)
+        def _():
+            downs[i]().start()
+
+    for copy in edges + sums:
+        copy.start()
+    start(0)
+
+    @pl.when(band == 0)
+    def _():
+        below_ref[...] = jnp.zeros_like(below_ref)
+        sum_below[...] = jnp.zeros_like(sum_below)
+
+    @pl.when(band == bands - 1)
+    def _():
+        above_ref[...] = jnp.zeros_like(above_ref)
+        sum_above[...] = jnp.zeros_like(sum_above)
+
+    for copy in edges:
+        copy.wait()
+    for ch in range(stack_ref.shape[0]):
+        own_ref[ch, :, :split_at] = stack_ref[ch, :, :split_at]
+        own_ref[ch, :, split_at:] = (
+            stack_ref[ch, :, split_at:].astype(jnp.float32)
+            + edge_left[ch].astype(jnp.float32)
+            + edge_right[ch].astype(jnp.float32)
+        ).astype(jnp.bfloat16)
+    start(1)
+
+    for copy in sums:
+        copy.wait()
+    at = atmos_cols - split_at
+
+    def settle(value, from_left, from_right):
+        lane = lax.broadcasted_iota(jnp.int32, from_left.shape, 1)
+        low = jnp.where(lane < reach, pltpu.roll(from_left, LANE - at, 1), 0.0)
+        mine = (lane >= at - reach) & (lane < at)
+        high = jnp.where(mine, pltpu.roll(from_right, LANE - 2 * reach, 1), 0.0)
+        if split_at == 0:
+            return value + low + high
+        middle = [value[:, LANE:split_at]] if split_at > LANE else []
+        return jnp.concatenate(
+            [value[:, :LANE] + low, *middle, value[:, split_at:] + high], axis=1
+        )
+
+    for i in (0, 2, 1):
+        for ch in range(2):
+            total[i, ch] = settle(part_refs[i][ch], part_left[i, ch], part_right[i, ch])
+        if i == 2:
+            start(2)
+    lon_sums = settle(ones_ref[...], ones_left[...], ones_right[...])[:1]
+
+    @pl.when(has_below)
+    def _():
+        ups[2]().wait_recv()
+
+    @pl.when(has_above)
+    def _():
+        downs[2]().wait_recv()
+
+    value = [total[1, ch] + sum_below[ch] + sum_above[ch] for ch in range(2)]
+    lat_sums = value[1][:, wide : wide + 1]
+    safe = jnp.maximum(value[1], FLOOR_SHARE * (lat_sums * lon_sums + 1.0))
+    surface_ref[...] = value[0] / safe
+
+    for i in range(2):
+
+        @pl.when(has_below)
+        def _():
+            ups[i]().wait_recv()
+
+        @pl.when(has_above)
+        def _():
+            downs[i]().wait_recv()
+
+    for i in range(3):
+
+        @pl.when(has_above)
+        def _():
+            ups[i]().wait_send()
+
+        @pl.when(has_below)
+        def _():
+            downs[i]().wait_send()
+
+
+def neighbours_call(stack, to_left, to_right, parts, ones, atmos_cols):
+    channels, rows, width = stack.shape
+    vmem = pl.BlockSpec(memory_space=pltpu.VMEM)
+    edge = pltpu.VMEM((channels, rows, LANE), jnp.bfloat16)
+    beside = pltpu.VMEM((3, 2, rows, LANE), jnp.float32)
+    column = pltpu.VMEM((8, LANE), jnp.float32)
+    block = pltpu.VMEM((2, rows, width), jnp.float32)
+    return pl.pallas_call(
+        lambda *refs: neighbours_kernel(atmos_cols, *refs),
+        out_shape=[jax.ShapeDtypeStruct(stack.shape, stack.dtype)] * 3
+        + [jax.ShapeDtypeStruct((rows, width), jnp.float32)],
+        in_specs=[vmem] * 7,
+        out_specs=[vmem] * 4,
+        scratch_shapes=[
+            edge,
+            edge,
+            beside,
+            beside,
+            column,
+            column,
+            pltpu.VMEM((3, 2, rows, width), jnp.float32),
+            block,
+            block,
+            pltpu.SemaphoreType.DMA((10,)),
+            pltpu.SemaphoreType.DMA((10,)),
+            pltpu.SemaphoreType.DMA((6,)),
+            pltpu.SemaphoreType.DMA((6,)),
+        ],
+        compiler_params=pltpu.CompilerParams(
+            collective_id=0, has_side_effects=True, vmem_limit_bytes=VMEM_LIMIT
+        ),
+        name="exchange_neighbours",
+    )(stack, to_left, to_right, *parts, ones)
+
+
+def neighbours_plan(rows, stack, field, flag_t, q, first_row, row_taps, row_sums, table):
+    chunk_table, chunk_total, atmos_cols = table
+    reach = LON_REACH
+    at = atmos_cols % LANE
+    assert reach <= at and at + 2 * reach < LANE
+    place = lambda edge, lane: jnp.pad(edge, ((0, 0), (0, 0), (lane, LANE - reach - lane)))
+    to_left = place(stack[:, :, :reach], at)
+    to_right = place(stack[:, :, atmos_cols - reach : atmos_cols], at + reach)
+    matrices = [row_matrix(first_row + d * rows, row_taps, rows) for d in (1, 0, -1)]
+    *parts, ones = backward_call(
+        field,
+        flag_t,
+        q,
+        [matrix.T.astype(jnp.bfloat16) for matrix in matrices],
+        chunk_table,
+        chunk_total,
+        atmos_cols + 2 * reach,
+    )
+    own, below, above, surface = neighbours_call(stack, to_left, to_right, parts, ones, atmos_cols)
+    ocean_flux = forward_call(
+        [below, own, above],
+        [matrix.astype(jnp.bfloat16) for matrix in matrices],
+        q,
+        chunk_table,
+        chunk_total,
+        row_sums,
+        flag_t,
+    )
+    return ocean_flux, surface[:, :atmos_cols]
+
+
 def exchange_plan(capacity, rows, stack, field, flag_t, q, first_row, row_taps, row_sums, table):
     chunk_table, chunk_total, atmos_cols = table
     reach = LON_REACH
@@ -242,6 +490,11 @@
     steps = -(-capacity // rows)
     tail = capacity - rows * (steps - 1)
     count = lambda t: tail if t == steps else rows
+
+    right = neighbour(stack[:, :, :reach], "lon", -1)
+    left = neighbour(stack[:, :, atmos_cols - reach : atmos_cols], "lon", 1)
+    filler = jnp.zeros(stack.shape[:2] + (stack.shape[2] - wide,), stack.dtype)
+    stack = jnp.concatenate([stack[:, :, :atmos_cols], right, left, filler], axis=2)
 
     around = {0: (0, rows)}
     pieces = {0: stack}
@@ -266,7 +519,7 @@
 
     def beside(start):
         edge = [part[:, :, start : start + reach] for part in parts]
-        edge.append(jnp.broadcast_to(ones[None, :, start : start + reach], (2, 1, reach)))
+        edge.append(jnp.broadcast_to(ones[None, :1, start : start + reach], (2, 1, reach)))
         return jnp.concatenate(edge, axis=1)
 
     from_left = neighbour(beside(atmos_cols), "lon", 1)
@@ -287,7 +540,7 @@
     for d, part in zip(order, parts):
         totals[d] = settle(part, row, part.shape[1])
         row += part.shape[1]
-    lon_sums = settle(jnp.broadcast_to(ones[None], (2, 1, width)), row, 1)[0, 0, :atmos_cols]
+    lon_sums = settle(jnp.broadcast_to(ones[None, :1], (2, 1, width)), row, 1)[0, 0, :atmos_cols]
 
     up, down = totals[steps], totals[-steps]
     for t in range(1, steps + 1):
@@ -344,11 +597,7 @@
     stack = jnp.concatenate(
         [exchange_density_arrays * water_atmos[None], water_atmos[None]], axis=0
     )
-    channels = stack.shape[0]
-    right = neighbour(stack[:, :, :reach], "lon", -1)
-    left = neighbour(stack[:, :, atmos_cols - reach :], "lon", 1)
-    filler = jnp.zeros((channels, atmos_rows, width - atmos_cols - 2 * reach), jnp.bfloat16)
-    stack = jnp.concatenate([stack, right, left, filler], axis=2)
+    stack = jnp.pad(stack, ((0, 0), (0, 0), (0, width - atmos_cols)))
 
     here = lambda array, pos, count: lax.dynamic_slice_in_dim(array, pos * count, count)
     row_taps = tap_weights(
@@ -381,6 +630,7 @@
     plans = [
         (lambda *operands, n=n: exchange_plan(n, atmos_rows, *operands, table)) for n in capacities
     ]
+    plans[0] = lambda *operands: neighbours_plan(atmos_rows, *operands, table)
     ocean_flux, surface = lax.switch(
         choice,
         plans,

time: 107 us -> 92.8 us (0.87)
  Pallas kernels: 22.6 us -> 62.9 us
  waiting for transfers between devices: 27.5 us -> 0 us
  starting transfers between devices: 18.6 us -> 0 us
  other arithmetic: 17.9 us -> 11.2 us
  local copies, waits for them, and re-layouts: 16.6 us -> 15.5 us
    pallas_call x0 -> x1, Pallas kernels: none -> 40.4 us  [neighbours_call(): pl.pallas_call(lambda *refs: neighbours_kernel(atmos_cols, *refs), out_sh...]
    ppermute x8 -> x0, waiting for transfers between devices: 27.5 us -> none  [the longest x4 16.3 us: shift(): return lax.ppermute(block, axis, pairs)]
    ppermute x8 -> x0, starting transfers between devices: 18.6 us -> none  [the longest x4 13.4 us: shift(): return lax.ppermute(block, axis, pairs)]
    unnamed x14 -> x11, local copies, waits for them, and re-layouts: 1.6 us -> 6.48 us
    slice x7 -> x1, local copies, waits for them, and re-layouts: 4.57 us -> 1.1 us  [neighbours_plan(): to_right = place(stack[:, :, atmos_cols - reach:atmos_cols], at + reach)]
    squeeze x1 -> x0, local copies, waits for them, and re-layouts: 3.13 us -> none  [local(): marine_thermal_frozen_values[0]]
    another operation x0 -> x1, local copies, waits for them, and re-layouts: none -> 2.98 us
    broadcast_in_dim x5, local copies, waits for them, and re-layouts: 3.01 us -> 0.63 us  [column_tiles(): result = result + jnp.where(offset == first + k, taps[k], jnp.float32(0.0))]
  transfers between devices with their start and end apart: 8 -> 0, of which waited for: 5 -> 0; matrix products, arithmetic and copies ran while one was open for 16% -> 0% of each run, Pallas kernels for 0% -> 0%
where the time goes in v1:
time: 92.8 us; the launch traced here: 91.8 us
  Pallas kernels  62.9 us (68%)
  local copies, waits for them, and re-layouts  15.5 us (17%)
  other arithmetic  11.2 us (12%)
  between operations  2.08 us (2%)
    pallas_call x1, Pallas kernels, neighbours_call(): pl.pallas_call(lambda *refs: neighbours_kernel(atmos_cols, *refs), out_sh...  40.4 us
    pallas_call x1, Pallas kernels, forward_call(): pl.pallas_call(lambda *refs: forward_kernel(blocks, *refs), out_shape=jax...  12.7 us
    pallas_call x1, Pallas kernels, backward_call(): pl.pallas_call(lambda *refs: backward_kernel(blocks, (ocean_rows, ocean_c...  9.82 us
    unnamed x11, local copies, waits for them, and re-layouts  6.48 us
    another operation x1, local copies, waits for them, and re-layouts  2.98 us
    convert_element_type x1, other arithmetic, column_tiles(): return result.astype(jnp.bfloat16)  2.32 us

profile of v1, /device:TPU:0, one launch (start us, length us, event | category | flops | bytes accessed | tf_op | source)
XLA Modules:
  0.0 91.8 jit_solution(6773896586284530995)
XLA Ops:
  0.6 0.8 reshape.230
  1.4 0.2 fusion.12
  1.6 0.6 subtract_reduce_fusion
  3.5 1.0 %fusion.36 = bf16[1,84,720]{2,1,0:T(8,128)(2,1)S(1)} fusion(s32[84,720]{1,0:T(8,128)} %param.22), kind=kLoop, calls=%fused_computation.301 | loop fusion | flops 120960 | bytes 362880 | tf_op jit(solution)/shard_map/broadcast_in_dim | solution.py:598
  4.5 1.0 %subtract_convert_fusion = bf16[84,720]{1,0:T(8,128)(2,1)S(1)} fusion(s32[84,720]{1,0:T(8,128)} %param.22), kind=kLoop, calls=%fused_computation.248 | loop fusion | flops 120960 | bytes 362880 | tf_op jit(solution)/shard_map/convert_element_type | solution.py:596
  5.5 1.2 %broadcast_multiply_fusion = bf16[6,84,720]{2,1,0:T(8,128)(2,1)S(1)} fusion(bf16[6,84,720]{2,1,0:T(8,128)(2,1)} %param.20, bf16[84,720]{1,0:T(8,128)(2,1)S(1)} %subtract_convert_fusion), kind=kLoop, calls=%fused_computation.247 | loop fusion | flops 362880 | bytes 1572480 | tf_op jit(solution)/shard_map/mul | solution.py:598
  6.7 1.1 %fusion.6 = bf16[7,84,768]{2,1,0:T(8,128)(2,1)} fusion(bf16[1,84,720]{2,1,0:T(8,128)(2,1)S(1)} %fusion.36, bf16[6,84,720]{2,1,0:T(8,128)(2,1)S(1)} %broadcast_multiply_fusion), kind=kLoop, calls=%fused_computation.246 | loop fusion | flops 3161088 | bytes 1749888 | tf_op jit(solution)/shard_map/concatenate | solution.py:597
  7.8 0.8 dynamic-slice_subtract_fusion
  8.6 0.8 dynamic_slice.19
  9.3 0.8 fusion.13
  10.2 6.4 %copy.208 = f32[1,252,2160]{1,2,0:T(8,128)} copy(f32[1,252,2160]{2,0,1:T(1,128)} %param.21) | data formatting | bytes 4354560 | tf_op args[1]
  17.1 0.6 broadcast_in_dim.525
  17.7 2.3 %add_convert_fusion.30 = bf16[9,256,256]{2,1,0:T(8,128)(2,1)S(1)} fusion(f32[9,256]{1,0:T(8,128)S(1)} %broadcast_in_dim.534, s32[9,256]{1,0:T(8,128)S(1)} %get-tuple-element.431, f32[9,256]{1,0:T(8,128)S(1)} %broadcast_in_dim.532, s32[9,256]{1,0:T(8,128)S(1)} %get-tuple-element.432, f32[9,256]{1,0:T(8,128)S(1)} %broadcast_in_dim.530, ...), kind=kLoop, calls=%fused_computation.242 | loop fusion | flops 8847360 | bytes 1281024 | tf_op jit(solution)/shard_map/convert_element_type | solution.py:68
  20.0 71.7 %conditional.1 = (bf16[6,2160,252]{2,1,0:T(8,128)(2,1)}, f32[1,84,720]{2,0,1:T(1,128)}) conditional(s32[]{:T(128)} %clamp.3, (bf16[7,84,768]{2,1,0:T(8,128)(2,1)}, s32[256]{0:T(256)S(1)}, f32[256,4]{0,1:T(4,128)S(1)}, s32[18]{0:T(128)S(1)}, f32[252,2160]{0,1:T(8,128)}, /*index=5*/s32[2160,252]{1,0:T(8,128)S(1)}, ...), branch_computations={%region_3.4_spmd, %region_4.5_spmd, %region_5.6_spmd} | conditional | flops 5143945216 | bytes 97440424 | solution.py:634
  20.1 1.1 %fusion.14 = (bf16[7,84,4]{2,1,0:T(8,128)(2,1)S(1)}, bf16[7,84,4]{2,1,0:T(8,128)(2,1)S(1)}) fusion(bf16[7,84,768]{2,1,0:T(8,128)(2,1)} %get-tuple-element.56.refs_0_), kind=kLoop, calls=%fused_computation.279 | loop fusion | bytes 18816 | tf_op jit(solution)/shard_map/cond/branch_0_fun/slice | solution.py:462
  21.2 0.8 pad.81.refs_1_
  22.0 0.8 pad.82.refs_2_
  22.7 3.0 %copy.209.refs_1_ = f32[252,2160]{1,0:T(8,128)} copy(f32[252,2160]{0,1:T(8,128)} %get-tuple-element.232) | data formatting | bytes 4354560 | tf_op jit(solution)/shard_map
  25.7 0.7 add_convert_fusion.3
  26.5 9.8 %fold_surface.3 = (f32[2,84,768]{2,1,0:T(8,128)}, f32[2,84,768]{2,1,0:T(8,128)}, f32[2,84,768]{2,1,0:T(8,128)}, f32[8,768]{1,0:T(8,128)}) custom-call(s32[18]{0:T(128)S(1)} %get-tuple-element.55.refs_0_, f32[252,2160]{1,0:T(8,128)} %copy.209.refs_1_, s32[2160,252]{1,0:T(8,128)S(1)} %get-tuple-element.59.refs_2_.refs_9_, ...), custom_call_target="tpu_custom_call" | custom-call | flops 905969664 | bytes 8388608 | tf_op jit(solution)/shard_map/cond/branch_0_fun/fold_surface/pallas_call | solution.py:214
  36.3 40.4 %exchange_neighbours.1 = (bf16[7,84,768]{2,1,0:T(8,128)(2,1)}, bf16[7,84,768]{2,1,0:T(8,128)(2,1)}, bf16[7,84,768]{2,1,0:T(8,128)(2,1)}, f32[84,768]{1,0:T(8,128)}) custom-call(bf16[7,84,768]{2,1,0:T(8,128)(2,1)S(1)} %copy-done.1, bf16[7,84,128]{2,1,0:T(8,128)(2,1)} %pad.81.refs_1_, bf16[7,84,128]{2,1,0:T(8,128)(2,1)} %pad.82.refs_2_, ...), custom_call_target="tpu_custom_call" | custom-call | tf_op jit(solution)/shard_map/cond/branch_0_fun/exchange_neighbours/pallas_call | solution.py:427
  76.7 1.4 %add_convert_fusion = (bf16[256,84]{1,0:T(8,128)(2,1)}, bf16[256,84]{1,0:T(8,128)(2,1)}, bf16[256,84]{1,0:T(8,128)(2,1)}) fusion(s32[256]{0:T(256)S(1)} %get-tuple-element.278, s32[256]{0:T(256)S(1)} %get-tuple-element.279, s32[256]{0:T(256)S(1)} %get-tuple-element.280, s32[256]{0:T(256)S(1)} %get-tuple-element.277, f32[256]{0:T(256)S(1)} %bitcast.91, ...), kind=kLoop, calls=%fused_computation.1 | loop fusion | flops 774144 | bytes 145408 | tf_op jit(solution)/shard_map/cond/branch_0_fun/convert_element_type | solution.py:476
  78.1 12.7 %spread_fluxes.3 = bf16[6,2160,252]{2,1,0:T(8,128)(2,1)} custom-call(s32[18]{0:T(128)S(1)} %get-tuple-element.55.refs_0_, bf16[7,84,768]{2,1,0:T(8,128)(2,1)} %get-tuple-element.67.refs_1_, bf16[7,84,768]{2,1,0:T(8,128)(2,1)} %get-tuple-element.68.refs_2_, bf16[7,84,768]{2,1,0:T(8,128)(2,1)} %get-tuple-element.69.refs_3_, ...), custom_call_target="tpu_custom_call" | custom-call | flops 4227858432 | bytes 16777216 | tf_op jit(solution)/shard_map/cond/branch_0_fun/spread_fluxes/pallas_call | solution.py:131
  90.8 1.0 %copy.213 = f32[1,84,720]{2,0,1:T(1,128)} copy(f32[1,84,720]{2,1,0:T(8,128)S(1)} %slice_bitcast_fusion) | data formatting | bytes 483840 | tf_op jit(solution)/shard_map/cond
  (31 shorter events, 0.5 us)
Async XLA Ops:
  7.8 8.8 %copy-start.89 = (s32[4320]{0:T(1024)S(1)}, s32[4320]{0:T(1024)}, u32[]{:S(2)}) copy-start(s32[4320]{0:T(1024)} %param.28) | copy-start | bytes 51844
  10.1 6.6 %copy-start.14 = (bf16[4320,5]{0,1:T(8,128)(2,1)S(1)}, bf16[4320,5]{0,1:T(8,128)(2,1)}, u32[]{:S(2)}) copy-start(bf16[4320,5]{0,1:T(8,128)(2,1)} %param.29) | copy-start | bytes 129604
  10.1 6.8 %copy-start.90 = (s32[4320]{0:T(1024)S(1)}, s32[4320]{0:T(1024)}, u32[]{:S(2)}) copy-start(s32[4320]{0:T(1024)} %param.27) | copy-start | bytes 51844
  10.1 9.9 %copy-start = (s32[252,2160]{0,1:T(8,128)S(1)}, s32[252,2160]{0,1:T(8,128)}, u32[]{:S(2)}) copy-start(s32[252,2160]{0,1:T(8,128)} %param.23) | copy-start | bytes 6531844
  10.1 9.9 %copy-start.84 = (s32[18]{0:T(128)S(1)}, s32[18]{0:T(128)}, u32[]{:S(2)}) copy-start(s32[18]{0:T(128)} %constant.208.clone) | copy-start | bytes 220
  26.5 9.8 %copy-start.1 = (bf16[7,84,768]{2,1,0:T(8,128)(2,1)S(1)}, bf16[7,84,768]{2,1,0:T(8,128)(2,1)}, u32[]{:S(2)}) copy-start(bf16[7,84,768]{2,1,0:T(8,128)(2,1)} %get-tuple-element.56.refs_0_) | copy-start | bytes 2709508 | tf_op jit(solution)/shard_map/cond
  78.1 12.7 %copy-start.13 = (f32[84,768]{1,0:T(8,128)S(1)}, f32[84,768]{1,0:T(8,128)}, u32[]{:S(2)}) copy-start(f32[84,768]{1,0:T(8,128)} %get-tuple-element.71) | copy-start | bytes 774148 | tf_op jit(solution)/shard_map/cond
